TPU v7x, 256 devices: a whole 4x4x8 slice. The times are simulated.
256 devices in a mesh: dp: 16 (over z, core), mp: 4 (over y), pre: 4 (over x).
Axes of the slice: x: 4, y: 4, z: 8, core: 2. Of those that a mesh axis runs over, the one named last changes fastest.
Arguments:
- hidden: bfloat16 [16384, 6144], P(('dp', 'pre'), 'mp'), may hold values from -16 to 16
- grad_out: bfloat16 [16384, 8192], P(('dp', 'mp'), 'pre'), may hold values from -1 to 1
- block_owner: int32 [4, 4, 12, 1], P('mp', 'pre'), may hold values from 0 to 15; in each aligned block of 12 rows (0 to 11, 12 to 23, ..., all dimensions but the last counted through in order) at most 2 rows name the same one
- left_stat: bfloat16 [32, 2048, 2048], P('dp', 'mp', 'pre'), may hold values from -1 to 20, as said below
- right_stat: bfloat16 [32, 2048, 2048], P('dp', 'mp', 'pre'), may hold values from -1 to 20, as said below
- left_root: bfloat16 [32, 2048, 2048], P('dp', 'mp', 'pre'), may hold values from -1 to 2, as said below
- right_root: bfloat16 [32, 2048, 2048], P('dp', 'mp', 'pre'), may hold values from -1 to 2, as said below
Outputs:
- update: bfloat16 [6144, 8192], P('mp', 'pre')
Inputs may be any that keep to these rules, and one draw needn't show every extreme that they name: `block_owner`: within the 12 blocks of one cell (one device's blocks), no owner is named more than 2 times, a bound that some block reaches. `left_stat`: each 512 x 512 tile is symmetric positive definite. `right_stat`: each 512 x 512 tile is symmetric positive definite. `left_root`: each 512 x 512 tile is symmetric. `right_root`: each 512 x 512 tile is symmetric.
All inputs are finite; a program needn't handle non-finite values.
Results may differ from a plain program's by a relative error of at most 0.025.
Values may be sent and summed in bfloat16 or wider, within the bound.
A program may use at most 128 MiB of HBM per device.

v0:
```python
import jax
import jax.numpy as jnp
from jax import lax
from jax.sharding import PartitionSpec as P


def dot_high(left_arg, right_arg):
    return jnp.dot(
        left_arg, right_arg, precision=lax.Precision.HIGHEST, preferred_element_type=jnp.float32
    )


def inverse_root(root_tile, stat_tile):
    start = root_tile.astype(jnp.float32)
    square = dot_high(start, start)
    product = dot_high(square, stat_tile)
    fourth = dot_high(square, product)
    identity = jnp.eye(start.shape[0], dtype=jnp.float32)
    return dot_high(start, 5.0 * identity - fourth) * 0.25


def precondition(gradient, left_tile, right_tile, left_start, right_start):
    left_full = 0.8 * left_tile.astype(jnp.float32) + 0.2 * jnp.dot(
        gradient, gradient.T, preferred_element_type=jnp.float32
    )
    right_full = 0.8 * right_tile.astype(jnp.float32) + 0.2 * jnp.dot(
        gradient.T, gradient, preferred_element_type=jnp.float32
    )
    left_new = inverse_root(left_start, left_full)
    right_new = inverse_root(right_start, right_full)
    result = dot_high(dot_high(left_new, gradient.astype(jnp.float32)), right_new)
    inv_norm = lax.rsqrt(jnp.mean(result * result) + 1e-06)
    return (result * inv_norm).astype(jnp.bfloat16)


def shards(hidden, grad_out, block_owner, left_stat, right_stat, left_root, right_root):
    block_size = left_stat.shape[1]
    slot_count = left_stat.shape[0]
    learners = lax.axis_size("dp")
    hid_all = lax.all_gather(hidden, "pre", axis=0, tiled=True)
    rows_cell = hid_all.shape[1]
    cols_cell = grad_out.shape[1]
    row_blocks = rows_cell // block_size
    col_blocks = cols_cell // block_size
    block_count = row_blocks * col_blocks
    partial_value = lax.dot_general(
        hid_all,
        lax.all_gather(grad_out, "mp", axis=0, tiled=True),
        (((0,), (0,)), ((), ())),
        preferred_element_type=jnp.float32,
    )
    owners = block_owner.reshape(block_count)
    indices = jnp.arange(block_count, dtype=jnp.int32)
    matches = (owners[:, None] == owners[None, :]) & (indices[None, :] < indices[:, None])
    position = jnp.sum(matches.astype(jnp.int32), axis=1)
    owner_ids = jnp.arange(learners, dtype=jnp.int32)
    slot_ids = jnp.arange(slot_count, dtype=jnp.int32)
    chosen = (owners[None, None, :] == owner_ids[:, None, None]) & (
        position[None, None, :] == slot_ids[None, :, None]
    )
    select = chosen.astype(jnp.bfloat16).reshape(learners, slot_count, row_blocks, col_blocks)
    summed = lax.psum(partial_value.astype(jnp.bfloat16), "dp")
    stacked = summed.reshape(row_blocks, block_size, col_blocks, block_size)
    own_select = lax.dynamic_index_in_dim(select, lax.axis_index("dp"), 0, keepdims=False)
    my_grads = jnp.einsum(
        "sxy,xiyj->sij", own_select, stacked, preferred_element_type=jnp.float32
    ).astype(jnp.bfloat16)
    results = jax.vmap(precondition)(my_grads, left_stat, right_stat, left_root, right_root)
    flat_select = select.reshape(learners * slot_count, row_blocks, col_blocks)
    cell_sum = jnp.einsum(
        "kxy,kij->xiyj",
        flat_select,
        lax.all_gather(results, "dp", axis=0, tiled=True),
        preferred_element_type=jnp.float32,
    )
    update = cell_sum.astype(jnp.bfloat16).reshape(rows_cell, cols_cell)
    return update


def solution(mesh):
    in_specs = (
        P(("dp", "pre"), "mp"),
        P(("dp", "mp"), "pre"),
        P("mp", "pre", None, None),
        P("dp", "mp", "pre"),
        P("dp", "mp", "pre"),
        P("dp", "mp", "pre"),
        P("dp", "mp", "pre"),
    )
    out_specs = P("mp", "pre")
    return jax.shard_map(shards, mesh=mesh, in_specs=in_specs, out_specs=out_specs, check_vma=False)
```

profile of v0, /device:TPU:1, one launch (start us, length us, event | category | flops | bytes accessed | tf_op | source)
XLA Modules:
  0.0 438.9 jit_solution(7741674563747663929)
XLA Ops:
  6.5 0.0 copy-start
  6.5 0.0 all-gather.4.cloned.1.call-start
  6.5 0.7 all-gather.4.cloned.1.call-update
  7.3 0.0 all-gather.6.cloned.1.call-start
  7.3 0.7 all-gather.6.cloned.1.call-update
  8.0 0.0 all-reduce.2.cloned.1.call-start
  8.1 47.0 %all-gather.4.cloned.1.call-done = bf16[1024,1536]{1,0:T(8,128)(2,1)} async-done(((bf16[256,1536]{1,0:T(8,128)(2,1)}), bf16[1024,1536]{1,0:T(8,128)(2,1)}) %all-gather.4.cloned.1.call-update) | async-done | bytes 3145744 | tf_op jit(solution)/shard_map/all_gather | solution.py:40
  55.1 52.9 %all-gather.6.cloned.1.call-done = bf16[1024,2048]{1,0:T(8,128)(2,1)} async-done(((bf16[256,2048]{1,0:T(8,128)(2,1)}), bf16[1024,2048]{1,0:T(8,128)(2,1)}) %all-gather.6.cloned.1.call-update) | async-done | bytes 4194320 | tf_op jit(solution)/shard_map/all_gather | solution.py:48
  108.0 11.3 %convolution_convert_fusion = bf16[1536,2048]{1,0:T(8,128)(2,1)} fusion(bf16[1024,1536]{1,0:T(8,128)(2,1)} %all-gather.4.cloned.1.call-done, bf16[1024,2048]{1,0:T(8,128)(2,1)} %all-gather.6.cloned.1.call-done), kind=kOutput, calls=%fused_computation.2 | convolution fusion | flops 6445596672 | bytes 13631488 | tf_op jit(solution)/shard_map/dot_general | solution.py:46
  119.3 11.1 %reshape.88 = bf16[3,512,4,512]{3,2,1,0:T(4,128)(2,1)} reshape(bf16[1536,2048]{1,0:T(8,128)(2,1)} %convolution_convert_fusion) | data formatting | bytes 12582912 | tf_op jit(solution)/shard_map/reshape | solution.py:63
  130.4 7.6 %copy.29 = bf16[3,512,4,512]{3,2,0,1:T(4,128)(2,1)} copy(bf16[3,512,4,512]{3,2,1,0:T(4,128)(2,1)} %reshape.88) | data formatting | bytes 12582912 | tf_op jit(solution)/shard_map/reshape | solution.py:63
  138.1 0.0 copy-start.8
  138.1 0.0 all-reduce.2.cloned.1.call-update
  138.1 0.2 all-gather.8.cloned.1.call-start
  138.3 0.5 broadcast.117
  138.8 0.0 copy-done.8
  138.8 0.6 reduce.3
  139.5 0.2 convert_reduce_fusion
  139.7 0.1 eq.88
  139.7 0.1 eq.80
  139.9 1.2 fusion.30
  141.1 0.0 copy-done
  141.1 0.0 copy-start.3
  141.1 2.1 fusion.46
  143.1 0.0 copy-done.3
  143.1 0.7 fusion.48
  143.9 122.0 %all-reduce.2.cloned.1.call-done = bf16[3,512,4,512]{3,2,0,1:T(4,128)(2,1)} async-done(((bf16[3,512,4,512]{3,2,0,1:T(4,128)(2,1)}), bf16[3,512,4,512]{3,2,0,1:T(4,128)(2,1)}) %all-reduce.2.cloned.1.call-update) | async-done | bytes 6291472 | tf_op jit(solution)/shard_map/psum | solution.py:62
  265.8 7.5 %bitcast_convert_fusion = bf16[2,512,512]{2,0,1:T(2,128)(2,1)S(1)} fusion(bf16[3,512,4,512]{3,2,0,1:T(4,128)(2,1)} %all-reduce.2.cloned.1.call-done, pred[2,3,4]{2,1,0:T(4,128)(4,1)S(1)} %and_bitcast_fusion), kind=kOutput, calls=%fused_computation.4 | convolution fusion | flops 13107200 | bytes 7340056 | tf_op jit(solution)/shard_map/sxy,xiyj->sij/dot_general | solution.py:65
  273.3 0.8 fusion.33
  274.0 0.0 copy-start.2
  274.0 0.0 copy-start.6
  274.0 0.8 fusion.31
  274.8 0.8 copy-done.2
  275.6 0.3 copy-done.6
  275.9 3.7 fusion.17
  279.6 0.0 copy-start.5
  279.6 3.8 fusion.47
  283.4 0.0 copy-done.5
  283.4 3.5 fusion.15
  287.0 0.0 copy-start.7
  287.0 1.9 fusion.13
  288.9 0.0 copy-done.7
  288.9 3.7 fusion.8
  292.7 0.0 copy-start.4
  292.7 3.6 fusion.49
  296.2 0.0 copy-done.4
  296.2 4.0 fusion.6
  300.2 3.8 multiply_reduce_fusion
  304.0 1.3 multiply_convert_fusion
  305.3 0.0 all-gather.8.cloned.1.call-update
  305.4 0.1 and.35
  305.5 0.1 copy.40
  305.6 96.5 %all-gather.8.cloned.1.call-done = bf16[32,512,512]{2,1,0:T(8,128)(2,1)} async-done(((bf16[2,512,512]{2,1,0:T(8,128)(2,1)}), bf16[32,512,512]{2,1,0:T(8,128)(2,1)}) %all-gather.8.cloned.1.call-update) | async-done | bytes 16777232 | tf_op jit(solution)/shard_map/all_gather | solution.py:73
  402.1 17.0 %convert_bitcast_fusion = bf16[3,512,4,512]{3,2,0,1:T(4,128)(2,1)S(1)} fusion(bf16[32,512,512,1]{2,1,0,3:T(8,128)(2,1)} %bitcast.35, pred[32,3,4]{0,2,1:T(4,128)(4,1)S(1)} %copy.40), kind=kOutput, calls=%fused_computation.3 | convolution fusion | flops 204472320 | bytes 23069056 | tf_op jit(solution)/shard_map/kxy,kij->xiyj/dot_general | solution.py:70
  419.0 4.8 %copy.41 = bf16[3,512,4,512]{3,2,1,0:T(4,128)(2,1)} copy(bf16[3,512,4,512]{3,2,0,1:T(4,128)(2,1)S(1)} %convert_bitcast_fusion) | data formatting | bytes 12582912 | tf_op jit(solution)/shard_map/convert_element_type | solution.py:76
  423.9 0.0 copy-start.1
  423.9 8.3 %copy.49 = bf16[192,8,4,512]{3,1,2,0:T(8,128)(2,1)} copy(bf16[192,8,4,512]{3,2,1,0:T(4,128)(2,1)} %bitcast.36) | data formatting | bytes 12582912
  432.1 0.0 copy-done.1
  (8 shorter events, 0.1 us)
Async XLA Ops:
  6.5 134.5 %copy-start = (bf16[2,512,512]{2,1,0:T(8,128)(2,1)S(1)}, bf16[2,512,512]{2,1,0:T(8,128)(2,1)}, u32[]{:S(2)}) copy-start(bf16[2,512,512]{2,1,0:T(8,128)(2,1)} %param.12) | copy-start | bytes 3145732
  6.5 48.5 %all-gather.4.cloned.1.call-start = ((), (), s32[]{:S(2)}) async-start(), calls=%async_computation | async-start | bytes 3932160 | tf_op jit(solution)/shard_map/all_gather | solution.py:40
  7.3 100.7 %all-gather.6.cloned.1.call-start = ((), (), s32[]{:S(2)}) async-start(), calls=%async_computation.1 | async-start | bytes 5242880 | tf_op jit(solution)/shard_map/all_gather | solution.py:48
  8.0 257.8 %all-reduce.2.cloned.1.call-start = ((), (), s32[]{:S(2)}) async-start(), calls=%async_computation.2 | async-start | bytes 12582912 | tf_op jit(solution)/shard_map/psum | solution.py:62
  138.1 0.8 copy-start.8
  138.1 264.0 %all-gather.8.cloned.1.call-start = ((), (), s32[]{:S(2)}) async-start(), calls=%async_computation.3 | async-start | bytes 17825792 | tf_op jit(solution)/shard_map/all_gather | solution.py:73
  141.1 2.1 copy-start.3
  274.0 1.6 copy-start.2
  274.0 1.8 copy-start.6
  279.6 3.8 copy-start.5
  287.0 1.9 copy-start.7
  292.7 3.6 copy-start.4
  423.9 8.3 %copy-start.1 = (bf16[2,512,512]{2,1,0:T(8,128)(2,1)S(1)}, bf16[2,512,512]{2,1,0:T(8,128)(2,1)}, u32[]{:S(2)}) copy-start(bf16[2,512,512]{2,1,0:T(8,128)(2,1)} %param.12) | copy-start | bytes 3145732
Sparse Core Ops, SparseCore 0:
  9.2 45.8 all-gather.3
  56.9 51.0 all-gather.5
  138.2 127.5 all-reduce.1
  305.5 96.5 all-gather.7
where the time goes:
time: 444 us; the launch traced here: 439 us
  waiting for transfers between devices  320 us (72%)
  matrix products  68 us (15%)
  local copies, waits for them, and re-layouts  33.9 us (8%)
  between operations  13.6 us (3%)
    psum x1, waiting for transfers between devices, shards(): summed = lax.psum(partial_value.astype(jnp.bfloat16), 'dp')  122 us
    all_gather x1, waiting for transfers between devices, shards(): lax.all_gather(results, 'dp', axis=0, tiled=True)  96.5 us
    all_gather x1, waiting for transfers between devices, shards(): lax.all_gather(grad_out, 'mp', axis=0, tiled=True)  52.9 us
    all_gather x1, waiting for transfers between devices, shards(): hid_all = lax.all_gather(hidden, 'pre', axis=0, tiled=True)  47 us
    dot_general x10, matrix products, dot_high(): jnp.dot(left_arg, right_arg, precision=lax.Precision.HIGHEST, preferred_e...  30.7 us
    reshape x2, local copies, waits for them, and re-layouts, shards(): stacked = summed.reshape(row_blocks, block_size, col_blocks, block_size)  18.8 us
    dot_general x1, matrix products, shards(): jnp.einsum('kxy,kij->xiyj', flat_select, lax.all_gather(results, 'dp', ax...  17 us
    dot_general x1, matrix products, shards(): lax.dot_general(hid_all, lax.all_gather(grad_out, 'mp', axis=0, tiled=Tru...  11.3 us
  transfers between devices with their start and end apart: 4, of which 4 were waited for; matrix products, arithmetic and copies ran while one was open for 1% of the time, Pallas kernels for 0%

commit v1 on v0

v1 whole, which is shorter than its diff:
```python
import functools

import jax
import jax.numpy as jnp
from jax import lax
from jax.experimental import pallas as pl
from jax.experimental.pallas import tpu as pltpu
from jax.sharding import PartitionSpec as P

MESH = pl.DeviceIdType.MESH
F32 = jnp.float32
BF16 = jnp.bfloat16

BLOCK = 512
BR = 3
BC = 4
NB = BR * BC
CAP = 2
CHIPS = 8
TOK = 256

Q = 2
U = 2
ROWS = BLOCK // 4 // Q
M = NB * Q + 4 * U
LAGS = sorted({max(n * Q, U) for n in range(2 * CAP + 1)})

T_RS = 0
T_RSLAG = T_RS + 2 * M
T_FIN = T_RSLAG + 2
T_KSLOT = T_FIN + 2 * 4
T_AG = T_KSLOT + 4
T_AGLAG = T_AG + M
T_LEN = T_AGLAG + 1


def tables(owners, chip):
    k = jnp.arange(NB, dtype=jnp.int32)
    dest = owners // 2
    same_owner = (owners[:, None] == owners[None, :]) & (k[None, :] < k[:, None])
    slot = jnp.sum(same_owner.astype(jnp.int32), axis=1)
    same_chip = (dest[:, None] == dest[None, :]) & (k[None, :] < k[:, None])
    rank = jnp.sum(same_chip.astype(jnp.int32), axis=1)
    chips = jnp.arange(CHIPS, dtype=jnp.int32)
    count = jnp.sum((dest[None, :] == chips[:, None]).astype(jnp.int32), axis=1)
    places = jnp.maximum(count * Q, U)

    def before(start, target, sigma):
        gap = ((start - target) * sigma) % CHIPS
        gaps = ((start - chips) * sigma) % CHIPS
        return jnp.sum(jnp.where(gaps[None, :] < gap[:, None], places[None, :], 0), axis=1)

    piece = jnp.arange(Q, dtype=jnp.int32)
    j = jnp.arange(M, dtype=jnp.int32)
    code = (k[:, None] * Q + piece[None, :]).reshape(-1)
    rs, rslag, fin, pos = [], [], [], []
    local = owners % 2 * CAP + slot
    slots = jnp.arange(4, dtype=jnp.int32)
    here = (dest == chip)[None, :] & (local[None, :] == slots[:, None])
    own_places = jnp.sum(jnp.where(chips == chip, places, 0))
    for sigma in (1, -1):
        up = (chip - sigma) % CHIPS
        at = before((chip - sigma) % CHIPS, dest, sigma) + rank * Q
        at = (at[:, None] + piece[None, :]).reshape(-1)
        rs.append(jnp.sum(jnp.where(at[None, :] == j[:, None], code[None, :], 0), axis=1))
        rslag.append(jnp.sum(jnp.where(chips == up, places, 0))[None])
        last = before((up - sigma) % CHIPS, dest, sigma) + rank * Q
        fin.append(jnp.sum(jnp.where(here, last[None, :], 0), axis=1))
        arrive = before(up, dest, sigma) + rank * Q
        pos.append(jnp.where(dest == chip, M + local * Q, arrive))
    kslot = jnp.sum(jnp.where(here, k[None, :], 0), axis=1)
    own_at = (rank[:, None] * Q + piece[None, :]).reshape(-1)
    own_code = (local[:, None] * Q + piece[None, :]).reshape(-1)
    own_here = jnp.repeat(dest == chip, Q)
    ag = jnp.sum(
        jnp.where((own_at[None, :] == j[:, None]) & own_here[None, :], own_code[None, :], 0), axis=1
    )
    table = jnp.concatenate(rs + rslag + fin + [kslot, ag, own_places[None]])
    return table.astype(jnp.int32), jnp.concatenate(pos).astype(jnp.int32)


def split(value):
    high = value.astype(BF16)
    return high, (value - high.astype(F32)).astype(BF16)


def mm(a, b):
    return jnp.dot(a, b, preferred_element_type=F32)


def mm_t(a, b):
    return lax.dot_general(a, b, (((0,), (0,)), ((), ())), preferred_element_type=F32)


def fifth(x, stat):
    sh, sl = split(mm(x, x))
    qh, ql = split(mm(sh, sh) + mm(sh, sl) + mm(sl, sh))
    x5 = mm(qh, x) + mm(ql, x)
    h, low = split(x5)
    return 1.25 * x.astype(F32) - 0.2 * (mm(h, stat) + mm(low, stat)), 0.05 * x5


def main_kernel(
    tab, hid, gro, ls, rs, lr, rr, out,
    hb, gb, pb, eb, sb, ssend, srecv, arecv, gfull, gx, own4, res, stats, ops, cf,
    local_sem, x_send, x_recv, y_send, y_recv, pe_send, pe_recv,
    s_send, s_recv, a_send, a_recv, gx_send, gx_recv, o_send, o_recv,
    f_local, f_send, f_recv, t_local, t_send, t_recv,
):
    dp = lax.axis_index("dp")
    mp = lax.axis_index("mp")
    pre = lax.axis_index("pre")
    chip = dp // 2
    core = lax.rem(dp, 2)
    mate = 1 - core
    peer = {"dp": chip * 2 + mate}
    x_to = [{"pre": lax.rem(pre + 1, 4)}, {"pre": lax.rem(pre + 3, 4)}]
    y_to = [{"mp": lax.rem(mp + 1, 4)}, {"mp": lax.rem(mp + 3, 4)}]
    z_to = [
        {"dp": lax.rem(chip + 1, CHIPS) * 2 + core},
        {"dp": lax.rem(chip + CHIPS - 1, CHIPS) * 2 + core},
    ]

    def remote(src, dst, send, recv, to):
        return pltpu.make_async_remote_copy(
            src_ref=src, dst_ref=dst, send_sem=send, recv_sem=recv, device_id=to, device_id_type=MESH
        )

    locals_ = []
    for i, src in enumerate((ls, rs, lr, rr)):
        locals_.append(pltpu.make_async_copy(src, stats.at[i], local_sem.at[i]))
    for r in range(BR):
        locals_.append(
            pltpu.make_async_copy(
                hid.at[:, pl.ds(r * BLOCK, BLOCK)], hb.at[r, pl.ds(pre * TOK, TOK)], local_sem.at[4 + r]
            )
        )
    for c in range(BC):
        locals_.append(
            pltpu.make_async_copy(
                gro.at[:, pl.ds(c * BLOCK, BLOCK)], gb.at[c, pl.ds(mp * TOK, TOK)], local_sem.at[7 + c]
            )
        )
    for copy in locals_:
        copy.start()

    barrier = pltpu.get_barrier_semaphore()
    for to in [peer] + x_to + y_to + z_to:
        pl.semaphore_signal(barrier, inc=1, device_id=to, device_id_type=MESH)
    pl.semaphore_wait(barrier, 7)

    def gather(src, buf, me, to, send, recv):
        def direct(i, way):
            return remote(
                src.at[:, pl.ds(i * BLOCK, BLOCK)],
                buf.at[i, pl.ds(me * TOK, TOK)],
                send.at[i, way], recv.at[i, way], to[way],
            )

        def arrived(i, way):
            who = lax.rem(me + (3 if way == 0 else 1), 4)
            part = buf.at[i, pl.ds(who * TOK, TOK)]
            return remote(part, part, send.at[i, way], recv.at[i, way], to[way])

        def forward(i, way):
            who = lax.rem(me + (3 if way == 0 else 1), 4)
            part = buf.at[i, pl.ds(who * TOK + way * (TOK // 2), TOK // 2)]
            return remote(part, part, send.at[i, 2 + way], recv.at[i, 2 + way], to[way])

        def far(i, way):
            who = lax.rem(me + 2, 4)
            part = buf.at[i, pl.ds(who * TOK + way * (TOK // 2), TOK // 2)]
            return remote(part, part, send.at[i, 2 + way], recv.at[i, 2 + way], to[way])

        return direct, arrived, forward, far

    rings = [
        (BR, gather(hid, hb, pre, x_to, x_send, x_recv)),
        (BC, gather(gro, gb, mp, y_to, y_send, y_recv)),
    ]

    def start_direct(i):
        for count, (direct, _, _, _) in rings:
            if i < count:
                for way in range(2):
                    direct(i, way).start()

    def pass_on(i):
        for count, (_, arrived, forward, _) in rings:
            if i < count:
                for way in range(2):
                    arrived(i, way).wait_recv()
                    forward(i, way).start()

    def finish(i):
        for count, (_, _, _, far) in rings:
            if i < count:
                for way in range(2):
                    far(i, way).wait_recv()

    def operators(side, s):
        a, b = fifth(stats[2 + side, s], stats[side, s])
        if side == 0:
            ops[s, 0], ops[s, 1] = split(a)
            ops[s, 2], ops[s, 3] = split(b)
        else:
            cf[s] = a
            ops[s, 4], ops[s, 5] = split(b)

    def to_mate(k):
        return remote(pb.at[k, mate], eb.at[k], pe_send.at[k], pe_recv.at[k], peer)

    def partial(r, c):
        k = r * BC + c
        value = mm_t(hb[r], gb[c]).astype(BF16)
        pb[k] = value.reshape(2, 2 * Q, ROWS, BLOCK)
        to_mate(k).start()

    def chunk_products(i):
        if i < BR:
            lax.fori_loop(0, i + 1, lambda c, _: (partial(i, c), 0)[1], 0)
        if i > 0:
            lax.fori_loop(0, min(i, BR), lambda r, _: (partial(r, i), 0)[1], 0)

    start_direct(0)
    start_direct(1)
    for copy in locals_[:4]:
        copy.wait()
    units = [(0, 0), (1, 0), (0, 1), (1, 1)]
    operators(*units[0])
    for copy in locals_[4:]:
        copy.wait()
    for i in range(BC):
        pass_on(i)
        if i + 2 < BC:
            start_direct(i + 2)
        if i + 1 < len(units):
            operators(*units[i + 1])
        finish(i)
        chunk_products(i)

    def add_halves(k, _):
        to_mate(k).wait_recv()
        for way in range(2):
            total = pb[k, core, pl.ds(way * Q, Q)].astype(F32) + eb[k, pl.ds(way * Q, Q)].astype(F32)
            sb[way, pl.ds(k * Q, Q)] = total.astype(BF16)
        return 0

    lax.fori_loop(0, NB, add_halves, 0)

    def s_copy(way, j):
        return remote(ssend.at[way, j], srecv.at[way, j], s_send.at[way, j], s_recv.at[way, j], z_to[way])

    def a_copy(way, j):
        return remote(ssend.at[way, j], arecv.at[way, j], a_send.at[way, j], a_recv.at[way, j], z_to[way])

    def delayed(buf, way, j, lag):
        value = buf[way, lax.max(j - LAGS[0], 0)]
        for candidate in LAGS[1:]:
            value = jnp.where(lag == candidate, buf[way, lax.max(j - candidate, 0)], value)
        return value

    def reduce_step(j, first):
        for way in range(2):
            own = sb[way, tab[T_RS + way * M + j]]
            if first:
                ssend[way, j] = own
            else:
                s_copy(way, j - U).wait_recv()
                lag = tab[T_RSLAG + way]
                came = delayed(srecv, way, j, lag).astype(F32)
                total = own.astype(F32) + jnp.where(j >= lag, came, 0.0)
                ssend[way, j] = total.astype(BF16)
            s_copy(way, j).start()

    for j in range(U):
        reduce_step(j, True)
    lax.fori_loop(U, M, lambda j, _: (reduce_step(j, False), 0)[1], 0)
    for way in range(2):
        for j in range(M - U, M):
            s_copy(way, j).wait_recv()

    def final(way, place, i):
        came = srecv[way, tab[T_FIN + way * 4 + place] + i].astype(F32)
        own = sb[way, tab[T_KSLOT + place] * Q + i].astype(F32)
        return (came + own).astype(BF16)

    def gx_copy(s):
        return remote(gx.at[s], gfull.at[s, core], gx_send.at[s], gx_recv.at[s], peer)

    for s in range(CAP):
        for way in range(2):
            for i in range(Q):
                gx[s, way * Q + i] = final(way, mate * CAP + s, i)
        gx_copy(s).start()
    for s in range(CAP):
        for way in range(2):
            for i in range(Q):
                gfull[s, core, way * Q + i] = final(way, core * CAP + s, i)

    def drain(j, _):
        for way in range(2):
            s_copy(way, j).wait_send()
        return 0

    def o_copy(s):
        place = core * CAP + s
        return remote(res.at[s, mate], own4.at[place], o_send.at[s], o_recv.at[s], peer)

    def o_arrive(s):
        place = mate * CAP + s
        return remote(res.at[s, mate], own4.at[place], o_send.at[s], o_recv.at[s], peer)

    for s in range(CAP):
        remote(gx.at[s], gfull.at[s, mate], gx_send.at[s], gx_recv.at[s], peer).wait_recv()
        g = gfull[s].reshape(BLOCK, BLOCK)
        gh, gl = split(mm_t(g, g))
        ggh, ggl = split(mm(g, gh) + mm(g, gl))
        m = mm(ops[s, 0], g) + mm(ops[s, 1], g)
        m = m - (mm(ops[s, 2], ggh) + mm(ops[s, 2], ggl) + mm(ops[s, 3], ggh))
        n = cf[s] - (mm(ops[s, 4], gh) + mm(ops[s, 4], gl) + mm(ops[s, 5], gh))
        mh, ml = split(m)
        nh, nl = split(n)
        p = mm(mh, nh) + mm(mh, nl) + mm(ml, nh)
        inv = lax.rsqrt(jnp.sum(p * p, keepdims=True) * (1.0 / (BLOCK * BLOCK)) + 1e-06)
        res[s] = (p * inv).astype(BF16).reshape(2, 2 * Q, ROWS, BLOCK)
        o_copy(s).start()
        own4[core * CAP + s] = res[s, core]

    lax.fori_loop(0, M, drain, 0)

    def f_here(way, j):
        return pltpu.make_async_copy(arecv.at[way, j], out.at[way, j, core], f_local.at[way, j])

    def f_mate(way, j, half):
        return remote(arecv.at[way, j], out.at[way, j, half], f_send.at[way, j], f_recv.at[way, j], peer)

    def t_here(way, place):
        return pltpu.make_async_copy(
            own4.at[place, pl.ds(way * Q, Q)], out.at[way, pl.ds(M + place * Q, Q), core], t_local.at[way, place]
        )

    def t_mate(way, place, half):
        return remote(
            own4.at[place, pl.ds(way * Q, Q)], out.at[way, pl.ds(M + place * Q, Q), half],
            t_send.at[way, place], t_recv.at[way, place], peer,
        )

    for s in range(CAP):
        o_arrive(s).wait_recv()

    def own_piece(way, j):
        code = tab[T_AG + j]
        return own4[code // Q, way * Q + lax.rem(code, Q)]

    def spread(way, j):
        f_here(way, j).start()
        f_mate(way, j, core).start()

    def gather_step(j, first):
        for way in range(2):
            own = own_piece(way, j)
            if first:
                ssend[way, j] = own
            else:
                a_copy(way, j - U).wait_recv()
                lag = tab[T_AGLAG]
                ssend[way, j] = jnp.where(j >= lag, delayed(arecv, way, j, lag), own)
            a_copy(way, j).start()
            if not first:
                spread(way, j - U)

    for j in range(U):
        gather_step(j, True)
    for way in range(2):
        for place in range(2 * CAP):
            t_here(way, place).start()
            t_mate(way, place, core).start()
    lax.fori_loop(U, M, lambda j, _: (gather_step(j, False), 0)[1], 0)
    for way in range(2):
        for j in range(M - U, M):
            a_copy(way, j).wait_recv()
            spread(way, j)

    def drain_all(j, _):
        for way in range(2):
            a_copy(way, j).wait_send()
            f_here(way, j).wait()
            f_mate(way, j, core).wait_send()
            f_mate(way, j, mate).wait_recv()
        return 0

    lax.fori_loop(0, M, drain_all, 0)
    for way in range(2):
        for place in range(2 * CAP):
            t_here(way, place).wait()
            t_mate(way, place, core).wait_send()
            t_mate(way, place, mate).wait_recv()
    for count, (direct, _, forward, _) in rings:
        for i in range(count):
            for way in range(2):
                direct(i, way).wait_send()
                forward(i, way).wait_send()
    lax.fori_loop(0, NB, lambda k, _: (to_mate(k).wait_send(), 0)[1], 0)
    for s in range(CAP):
        gx_copy(s).wait_send()
        o_copy(s).wait_send()


def run_main(table, hidden, grad_out, left_stat, right_stat, left_root, right_root):
    dma = pltpu.SemaphoreType.DMA
    anywhere = pl.BlockSpec(memory_space=pl.ANY)
    stream = pltpu.VMEM((2, M, ROWS, BLOCK), BF16)
    return pl.pallas_call(
        main_kernel,
        out_shape=jax.ShapeDtypeStruct((2, M + 4 * Q, 2, ROWS, BLOCK), BF16),
        in_specs=[pl.BlockSpec(memory_space=pltpu.SMEM)] + [anywhere] * 6,
        out_specs=anywhere,
        scratch_shapes=[
            pltpu.VMEM((BR, 4 * TOK, BLOCK), BF16),
            pltpu.VMEM((BC, 4 * TOK, BLOCK), BF16),
            pltpu.VMEM((NB, 2, 2 * Q, ROWS, BLOCK), BF16),
            pltpu.VMEM((NB, 2 * Q, ROWS, BLOCK), BF16),
            pltpu.VMEM((2, NB * Q, ROWS, BLOCK), BF16),
            stream,
            stream,
            stream,
            pltpu.VMEM((CAP, 2, 2 * Q, ROWS, BLOCK), BF16),
            pltpu.VMEM((CAP, 2 * Q, ROWS, BLOCK), BF16),
            pltpu.VMEM((2 * CAP, 2 * Q, ROWS, BLOCK), BF16),
            pltpu.VMEM((CAP, 2, 2 * Q, ROWS, BLOCK), BF16),
            pltpu.VMEM((4, CAP, BLOCK, BLOCK), BF16),
            pltpu.VMEM((CAP, 6, BLOCK, BLOCK), BF16),
            pltpu.VMEM((CAP, BLOCK, BLOCK), F32),
            dma((11,)),
            dma((BR, 4)), dma((BR, 4)), dma((BC, 4)), dma((BC, 4)),
            dma((NB,)), dma((NB,)),
            dma((2, M)), dma((2, M)), dma((2, M)), dma((2, M)),
            dma((CAP,)), dma((CAP,)), dma((CAP,)), dma((CAP,)),
            dma((2, M)), dma((2, M)), dma((2, M)),
            dma((2, 2 * CAP)), dma((2, 2 * CAP)), dma((2, 2 * CAP)),
        ],
        compiler_params=pltpu.CompilerParams(
            collective_id=0, has_side_effects=True, vmem_limit_bytes=60 * 1024 * 1024
        ),
        name="main",
    )(table, hidden, grad_out, left_stat, right_stat, left_root, right_root)


def lay_out_kernel(pos, pieces, out, buf, in_sem, out_sem):
    def read(k, way):
        return pltpu.make_async_copy(
            pieces.at[way, pl.ds(pos[way * NB + k], Q)], buf.at[k, way], in_sem.at[k, way]
        )

    def write(k, half, way, i):
        r, c = k // BC, k % BC
        row = r * BLOCK + half * (BLOCK // 2) + way * (BLOCK // 4) + i * ROWS
        return pltpu.make_async_copy(
            buf.at[k, way, i, half],
            out.at[pl.ds(row, ROWS), pl.ds(c * BLOCK, BLOCK)],
            out_sem.at[k, half, way, i],
        )

    parts = [(half, way, i) for half in range(2) for way in range(2) for i in range(Q)]
    for k in range(NB):
        for way in range(2):
            read(k, way).start()
    for k in range(NB):
        for way in range(2):
            read(k, way).wait()
        for half, way, i in parts:
            write(k, half, way, i).start()
    for k in range(NB):
        for half, way, i in parts:
            write(k, half, way, i).wait()


def run_lay_out(pos, pieces):
    dma = pltpu.SemaphoreType.DMA
    return pl.pallas_call(
        lay_out_kernel,
        out_shape=jax.ShapeDtypeStruct((BR * BLOCK, BC * BLOCK), BF16),
        in_specs=[pl.BlockSpec(memory_space=pltpu.SMEM), pl.BlockSpec(memory_space=pl.ANY)],
        out_specs=pl.BlockSpec(memory_space=pl.ANY),
        scratch_shapes=[
            pltpu.VMEM((NB, 2, Q, 2, ROWS, BLOCK), BF16),
            dma((NB, 2)),
            dma((NB, 2, 2, Q)),
        ],
        compiler_params=pltpu.CompilerParams(vmem_limit_bytes=32 * 1024 * 1024),
        name="lay_out",
    )(pos, pieces)


def shards(hidden, grad_out, block_owner, left_stat, right_stat, left_root, right_root):
    table, pos = tables(block_owner.reshape(NB), lax.axis_index("dp") // 2)
    pieces = run_main(table, hidden, grad_out, left_stat, right_stat, left_root, right_root)
    return run_lay_out(pos, pieces)


def solution(mesh):
    in_specs = (
        P(("dp", "pre"), "mp"),
        P(("dp", "mp"), "pre"),
        P("mp", "pre", None, None),
        P("dp", "mp", "pre"),
        P("dp", "mp", "pre"),
        P("dp", "mp", "pre"),
        P("dp", "mp", "pre"),
    )
    return jax.shard_map(
        shards, mesh=mesh, in_specs=in_specs, out_specs=P("mp", "pre"), check_vma=False
    )
```

time: 444 us -> 214 us (0.48); the launches traced: 439 us -> 213 us
  waiting for transfers between devices: 320 us -> 0 us
  Pallas kernels: 0 us -> 203 us
  matrix products: 68 us -> 0 us
  local copies, waits for them, and re-layouts: 33.9 us -> 7.12 us
  between operations: 13.6 us -> 0.26 us
    pallas_call x0 -> x2, Pallas kernels: none -> 203 us  [the longest x1 198 us: run_main(): pl.pallas_call(main_kernel, out_shape=jax.ShapeDtypeStruct((2, M + 4 * Q,...]
    all_gather x3 -> x0, waiting for transfers between devices: 196 us -> none  [the longest x1 96.5 us: shards(): lax.all_gather(results, 'dp', axis=0, tiled=True)]
    psum x1 -> x0, waiting for transfers between devices: 122 us -> none  [shards(): summed = lax.psum(partial_value.astype(jnp.bfloat16), 'dp')]
    dot_general x15 -> x0, matrix products: 68 us -> none  [the longest x10 30.7 us: dot_high(): jnp.dot(left_arg, right_arg, precision=lax.Precision.HIGHEST, preferred_e...]
    reshape x2 -> x0, local copies, waits for them, and re-layouts: 18.8 us -> none  [shards(): stacked = summed.reshape(row_blocks, block_size, col_blocks, block_size)]
    unnamed x20 -> x2, local copies, waits for them, and re-layouts: 9.91 us -> 3.97 us
    convert_element_type x1 -> x0, local copies, waits for them, and re-layouts: 4.82 us -> none  [shards(): update = cell_sum.astype(jnp.bfloat16).reshape(rows_cell, cols_cell)]
  transfers between devices with their start and end apart: 4 -> 0, of which waited for: 4 -> 0; matrix products, arithmetic and copies ran while one was open for 1% -> 0% of each run, Pallas kernels for 0% -> 0%
where the time goes in v1:
time: 214 us; the launch traced here: 213 us
  Pallas kernels  203 us (95%)
  local copies, waits for them, and re-layouts  7.12 us (3%)
  other arithmetic  3.51 us (2%)
    pallas_call x1, Pallas kernels, run_main(): pl.pallas_call(main_kernel, out_shape=jax.ShapeDtypeStruct((2, M + 4 * Q,...  198 us
    pallas_call x1, Pallas kernels, run_lay_out(): pl.pallas_call(lay_out_kernel, out_shape=jax.ShapeDtypeStruct((BR * BLOCK...  4.73 us

profile of v1, /device:TPU:1, one launch (start us, length us, event | category | flops | bytes accessed | tf_op | source)
XLA Modules:
  0.0 213.5 jit_solution(11342297256348499681)
XLA Ops:
  0.0 0.9 convert_reduce_fusion.1
  0.9 0.7 and_select_fusion.6
  1.6 0.2 convert_reduce_fusion
  1.8 0.1 convert_reduce_fusion.2
  1.9 0.7 fusion.8
  2.7 0.1 select_reduce_fusion.3
  2.8 0.1 pad_add_fusion.pos
  2.9 0.1 select_reduce_fusion.7
  3.0 0.1 broadcast_in_dim.151
  3.1 0.1 and.233
  3.2 0.1 iota_add_fusion.3
  3.2 0.1 add.303
  3.3 0.1 iota_add_fusion.2
  3.4 0.1 add.307
  3.5 0.1 iota_add_fusion.4
  3.6 0.1 add.299
  3.7 0.1 select_reduce_fusion.1
  3.8 0.1 iota_add_fusion.1
  3.8 0.1 add.319
  3.9 0.1 iota_add_fusion
  4.0 0.1 add.323
  4.1 0.1 select_reduce_fusion
  4.2 2.6 %concatenate.7.tab = s32[111]{0:T(128)} concatenate(s32[32]{0:T(128)S(1)} %get-tuple-element.16, s32[32]{0:T(128)S(1)} %get-tuple-element.15, s32[1]{0:T(128)} %bitcast.1, s32[1]{0:T(128)} %bitcast.2, s32[4]{0:T(128)S(1)} %get-tuple-element.7, s32[4]{0:T(128)S(1)} %get-tuple-element.6, s32[4]{0:T(128)S(1)} %get-tuple-element.5, s32[32]{0:T(128)S(1)} %select_reduce_fusion, s32[1]{0:T(128)} %bitcast.3), dimensions={0} | concatenate | bytes 888 | tf_op jit(solution)/shard_map/concatenate | solution.py:78
  6.7 197.9 %main.1.pieces = bf16[2,40,2,64,512]{4,3,2,1,0:T(8,128)(2,1)} custom-call(s32[111]{0:T(128)} %concatenate.7.tab, bf16[256,1536]{1,0:T(8,128)(2,1)} %hid.1, bf16[256,2048]{1,0:T(8,128)(2,1)} %gro.1, bf16[2,512,512]{2,1,0:T(8,128)(2,1)} %ls.1, bf16[2,512,512]{2,1,0:T(8,128)(2,1)} %rs.1, bf16[2,512,512]{2,1,0:T(8,128)(2,1)} %lr.1, bf16[2,512,512]{2,1,0:T(8,128)(2,1)} %rr.1), custom_call_target="tpu_custom_call" | custom-call | tf_op jit(solution)/shard_map/main/pallas_call | solution.py:414
  204.6 0.0 copy-start
  204.6 4.0 %copy-done = bf16[2,40,2,64,512]{4,3,2,1,0:T(8,128)(2,1)S(1)} copy-done((bf16[2,40,2,64,512]{4,3,2,1,0:T(8,128)(2,1)S(1)}, bf16[2,40,2,64,512]{4,3,2,1,0:T(8,128)(2,1)}, u32[]{:S(2)}) %copy-start) | copy-done | bytes 10485784
  208.6 4.7 %lay_out.1 = bf16[1536,2048]{1,0:T(8,128)(2,1)} custom-call(s32[24]{0:T(128)S(1)} %pad_add_fusion.pos, bf16[2,40,2,64,512]{4,3,2,1,0:T(8,128)(2,1)S(1)} %copy-done), custom_call_target="tpu_custom_call" | custom-call | tf_op jit(solution)/shard_map/lay_out/pallas_call | solution.py:481
  (6 shorter events, 0.1 us)
Async XLA Ops:
  204.6 4.0 %copy-start = (bf16[2,40,2,64,512]{4,3,2,1,0:T(8,128)(2,1)S(1)}, bf16[2,40,2,64,512]{4,3,2,1,0:T(8,128)(2,1)}, u32[]{:S(2)}) copy-start(bf16[2,40,2,64,512]{4,3,2,1,0:T(8,128)(2,1)} %main.1.pieces) | copy-start | bytes 31457284

commit v2 on v1

v2 whole, which is shorter than its diff:
```python
import jax
import jax.numpy as jnp
from jax import lax
from jax.experimental import pallas as pl
from jax.experimental.pallas import tpu as pltpu
from jax.sharding import PartitionSpec as P

MESH = pl.DeviceIdType.MESH
F32 = jnp.float32
BF16 = jnp.bfloat16

BLOCK = 512
BR = 3
BC = 4
NB = BR * BC
CAP = 2
CHIPS = 8
TOK = 256

Q = 2
U = 3
ROWS = BLOCK // 4 // Q
Z = max(2 * CAP * Q, U)
M = NB * Q + 4 * U
B = 4
assert M % B == 0 and Q * 2 >= U


def split(value):
    high = value.astype(BF16)
    return high, (value - high.astype(F32)).astype(BF16)


def mm(a, b):
    return jnp.dot(a, b, preferred_element_type=F32)


def mm_t(a, b):
    return lax.dot_general(a, b, (((0,), (0,)), ((), ())), preferred_element_type=F32)


def fifth(x, stat):
    sh, sl = split(mm(x, x))
    qh, ql = split(mm(sh, sh) + mm(sh, sl) + mm(sl, sh))
    x5 = mm(qh, x) + mm(ql, x)
    h, low = split(x5)
    return 1.25 * x.astype(F32) - 0.2 * (mm(h, stat) + mm(low, stat)), 0.05 * x5


def total(terms):
    result = terms[0]
    for term in terms[1:]:
        result = result + term
    return result


def make_tables(owner_ref, chip, places_ref, before_ref, rs_ref, fin_ref, kslot_ref, ag_ref, lag_ref, pos_ref):
    i32 = jnp.int32
    owner = [owner_ref[k] for k in range(NB)]
    dest = [lax.div(o, 2) for o in owner]

    def ones(flags):
        return total([f.astype(i32) for f in flags]) if flags else jnp.int32(0)

    slot = [jnp.minimum(ones([owner[e] == owner[k] for e in range(k)]), CAP - 1) for k in range(NB)]
    rank = [jnp.minimum(ones([dest[e] == dest[k] for e in range(k)]), 2 * CAP - 1) for k in range(NB)]
    local = [lax.rem(owner[k], 2) * CAP + slot[k] for k in range(NB)]
    for d in range(CHIPS):
        places_ref[d] = jnp.clip(ones([dest[k] == d for k in range(NB)]) * Q, U, Z)
    mine = places_ref[chip]
    lag_ref[2] = mine
    here = [(dest[k] == chip).astype(i32) for k in range(NB)]
    for s in range(2 * CAP):
        kslot_ref[s] = jnp.minimum(
            total([here[k] * (local[k] == s).astype(i32) * k for k in range(NB)]), NB - 1
        )
    for way, sigma in enumerate((1, -1)):
        near = [places_ref[lax.rem(chip + CHIPS - g * sigma, CHIPS)] for g in range(CHIPS)]
        lag_ref[way] = near[1]
        running = jnp.int32(0)
        for g in range(1, CHIPS):
            before_ref[g] = running
            running = running + near[g]
        before_ref[0] = running
        spot = []
        for k in range(NB):
            gap = lax.rem((chip - dest[k]) * sigma + CHIPS, CHIPS)
            spot.append(before_ref[gap] + rank[k] * Q)
            pos_ref[way * NB + k] = jnp.where(here[k] == 1, M + local[k] * Q, jnp.minimum(spot[k], M - Q))
        for s in range(2 * CAP):
            last = total(
                [here[k] * (local[k] == s).astype(i32) * (running - near[1] + rank[k] * Q) for k in range(NB)]
            )
            fin_ref[way * 2 * CAP + s] = jnp.minimum(last, M - Q)

        def piece_of(j, _):
            codes = []
            for k in range(NB):
                off = j - spot[k]
                codes.append(jnp.where((off >= 0) & (off < Q), k * Q + off, 0))
            rs_ref[way * M + j] = jnp.minimum(total(codes), NB * Q - 1)
            return 0

        lax.fori_loop(0, M, piece_of, 0)
    for i in range(Z):
        codes = []
        for k in range(NB):
            off = i - Z + mine - rank[k] * Q
            codes.append(jnp.where((here[k] == 1) & (off >= 0) & (off < Q), local[k] * Q + off, 0))
        ag_ref[i] = jnp.minimum(total(codes), 2 * CAP * Q - 1)


def main_kernel(
    owner_ref, hid, gro, ls, rs, lr, rr, out, pos_ref,
    hb, gb, pb, eb, sb, ssend, srecv, arecv, shadow, gfull, gx, own4, res, stats, ops, cf,
    places_ref, before_ref, rs_ref, fin_ref, kslot_ref, ag_ref, lag_ref,
    local_sem, x_send, x_recv, y_send, y_recv, pe_send, pe_recv,
    s_send, s_recv, a_send, a_recv, gx_send, gx_recv, o_send, o_recv,
    f_local, f_send, f_recv, t_local, t_send, t_recv,
):
    dp = lax.axis_index("dp")
    mp = lax.axis_index("mp")
    pre = lax.axis_index("pre")
    chip = dp // 2
    core = lax.rem(dp, 2)
    mate = 1 - core
    peer = {"dp": chip * 2 + mate}
    x_to = [{"pre": lax.rem(pre + 1, 4)}, {"pre": lax.rem(pre + 3, 4)}]
    y_to = [{"mp": lax.rem(mp + 1, 4)}, {"mp": lax.rem(mp + 3, 4)}]
    z_to = [
        {"dp": lax.rem(chip + 1, CHIPS) * 2 + core},
        {"dp": lax.rem(chip + CHIPS - 1, CHIPS) * 2 + core},
    ]

    def remote(src, dst, send, recv, to):
        return pltpu.make_async_remote_copy(
            src_ref=src, dst_ref=dst, send_sem=send, recv_sem=recv, device_id=to, device_id_type=MESH
        )

    stat_copies = [
        pltpu.make_async_copy(src, stats.at[i], local_sem.at[i]) for i, src in enumerate((ls, rs, lr, rr))
    ]
    token_copies = []
    for i in range(BC):
        if i < BR:
            token_copies.append(
                pltpu.make_async_copy(
                    hid.at[:, pl.ds(i * BLOCK, BLOCK)], hb.at[i, pl.ds(pre * TOK, TOK)], local_sem.at[4 + i]
                )
            )
        token_copies.append(
            pltpu.make_async_copy(
                gro.at[:, pl.ds(i * BLOCK, BLOCK)], gb.at[i, pl.ds(mp * TOK, TOK)], local_sem.at[7 + i]
            )
        )
    for copy in token_copies + stat_copies:
        copy.start()

    barrier = pltpu.get_barrier_semaphore()
    for to in [peer] + x_to + y_to + z_to:
        pl.semaphore_signal(barrier, inc=1, device_id=to, device_id_type=MESH)
    pl.semaphore_wait(barrier, 7)

    def gather(src, buf, me, to, send, recv):
        def direct(i, way):
            return remote(
                src.at[:, pl.ds(i * BLOCK, BLOCK)],
                buf.at[i, pl.ds(me * TOK, TOK)],
                send.at[0], recv.at[i, way], to[way],
            )

        def arrived(i, way):
            who = lax.rem(me + (3 if way == 0 else 1), 4)
            part = buf.at[i, pl.ds(who * TOK, TOK)]
            return remote(part, part, send.at[0], recv.at[i, way], to[way])

        def forward(i, way):
            who = lax.rem(me + (3 if way == 0 else 1), 4)
            part = buf.at[i, pl.ds(who * TOK + way * (TOK // 2), TOK // 2)]
            return remote(part, part, send.at[0], recv.at[i, 2 + way], to[way])

        def far(i, way):
            who = lax.rem(me + 2, 4)
            part = buf.at[i, pl.ds(who * TOK + way * (TOK // 2), TOK // 2)]
            return remote(part, part, send.at[0], recv.at[i, 2 + way], to[way])

        return direct, arrived, forward, far

    rings = [
        (BR, gather(hid, hb, pre, x_to, x_send, x_recv)),
        (BC, gather(gro, gb, mp, y_to, y_send, y_recv)),
    ]

    def start_direct(i):
        for count, (direct, _, _, _) in rings:
            if i < count:
                for way in range(2):
                    direct(i, way).start()

    def pass_on(i):
        for count, (_, arrived, forward, _) in rings:
            if i < count:
                for way in range(2):
                    arrived(i, way).wait_recv()
                    forward(i, way).start()

    def finish(i):
        for count, (_, _, _, far) in rings:
            if i < count:
                for way in range(2):
                    far(i, way).wait_recv()

    def operators(side, s):
        a, b = fifth(stats[2 + side, s], stats[side, s])
        if side == 0:
            ops[s, 0], ops[s, 1] = split(a)
            ops[s, 2] = b.astype(BF16)
        else:
            cf[s] = a
            ops[s, 3] = b.astype(BF16)

    def to_mate(k):
        return remote(pb.at[k, mate], eb.at[k], pe_send.at[0], pe_recv.at[k], peer)

    def partial(r, c):
        k = r * BC + c
        value = mm_t(hb[r], gb[c]).astype(BF16)
        pb[k] = value.reshape(2, 2 * Q, ROWS, BLOCK)
        to_mate(k).start()

    def add_halves(r, c):
        k = r * BC + c
        to_mate(k).wait_recv()
        for way in range(2):
            both = pb[k, core, pl.ds(way * Q, Q)].astype(F32) + eb[k, pl.ds(way * Q, Q)].astype(F32)
            sb[way, pl.ds(k * Q, Q)] = both.astype(BF16)

    def for_chunk(i, what):
        if i < BR:
            lax.fori_loop(0, i + 1, lambda c, _: (what(i, c), 0)[1], 0)
        if i > 0:
            lax.fori_loop(0, min(i, BR), lambda r, _: (what(r, i), 0)[1], 0)

    def between(i):
        if i == 0:
            for copy in stat_copies:
                copy.wait()
            operators(0, 0)
        elif i == 1:
            operators(1, 0)
            for way in range(2):
                shadow[way, pl.ds(0, Z)] = jnp.zeros((Z, ROWS, BLOCK), BF16)
        elif i == 2:
            make_tables(
                owner_ref, chip, places_ref, before_ref, rs_ref, fin_ref, kslot_ref, ag_ref, lag_ref, pos_ref
            )
            operators(0, 1)
        elif i == 3:
            operators(1, 1)

    start_direct(0)
    start_direct(1)
    for copy in token_copies:
        copy.wait()
    between(0)
    for i in range(BC + 1):
        if i < BC:
            pass_on(i)
            if i + 2 < BC:
                start_direct(i + 2)
            if i + 1 < BC:
                between(i + 1)
        if i > 0:
            finish(i - 1)
            for_chunk(i - 1, partial)
        if i > 1:
            for_chunk(i - 2, add_halves)
    for_chunk(BC - 1, add_halves)

    def s_copy(way, j):
        return remote(ssend.at[way, j], srecv.at[way, j], s_send.at[way], s_recv.at[way, j], z_to[way])

    def a_copy(way, j):
        return remote(ssend.at[way, j], arecv.at[way, j], a_send.at[way], a_recv.at[way, j], z_to[way])

    def stream(copy, landed, message, after):
        def step(j, send):
            for way in range(2):
                copy(way, j).wait_recv()
                if send:
                    shadow[way, Z + j] = landed[way, j]
                    ssend[way, j + U] = message(way, j + U)
                    copy(way, j + U).start()

        def batch(b, _):
            for t in range(B):
                step(b * B + t, True)
            after(b)
            return 0

        for j in range(U):
            for way in range(2):
                ssend[way, j] = message(way, j)
                copy(way, j).start()
        whole = (M - U) // B
        lax.fori_loop(0, whole, batch, 0)
        for b in range(whole, M // B):
            for t in range(B):
                step(b * B + t, b * B + t + U < M)
            after(b)

    def reduced(way, j):
        own = sb[way, rs_ref[way * M + j]]
        came = shadow[way, Z + j - lag_ref[way]]
        return own + came

    stream(s_copy, srecv, reduced, lambda b: None)
    for way in range(2):
        remote(ssend.at[way], srecv.at[way], s_send.at[way], s_recv.at[way, 0], z_to[way]).wait_send()

    def final(way, place, i):
        came = srecv[way, fin_ref[way * 2 * CAP + place] + i].astype(F32)
        own = sb[way, kslot_ref[place] * Q + i].astype(F32)
        return (came + own).astype(BF16)

    def gx_copy(s):
        return remote(gx.at[s], gfull.at[s, core], gx_send.at[s], gx_recv.at[s], peer)

    def gx_arrive(s):
        return remote(gx.at[s], gfull.at[s, mate], gx_send.at[s], gx_recv.at[s], peer)

    for s in range(CAP):
        for way in range(2):
            for i in range(Q):
                gx[s, way * Q + i] = final(way, mate * CAP + s, i)
        gx_copy(s).start()
    for s in range(CAP):
        for way in range(2):
            for i in range(Q):
                gfull[s, core, way * Q + i] = final(way, core * CAP + s, i)

    def o_copy(s):
        place = core * CAP + s
        return remote(res.at[s, mate], own4.at[:, pl.ds(place * Q, Q)], o_send.at[s], o_recv.at[s], peer)

    def o_arrive(s):
        place = mate * CAP + s
        return remote(res.at[s, mate], own4.at[:, pl.ds(place * Q, Q)], o_send.at[s], o_recv.at[s], peer)

    for s in range(CAP):
        gx_arrive(s).wait_recv()
        g = gfull[s].reshape(BLOCK, BLOCK)
        gram = mm_t(g, g).astype(BF16)
        cube = mm(g, gram).astype(BF16)
        m = mm(ops[s, 0], g) + mm(ops[s, 1], g) - mm(ops[s, 2], cube)
        n = cf[s] - mm(ops[s, 3], gram)
        p = mm(m.astype(BF16), n.astype(BF16))
        inv = lax.rsqrt(jnp.sum(p * p, keepdims=True) * (1.0 / (BLOCK * BLOCK)) + 1e-06)
        res[s] = (p * inv).astype(BF16).reshape(2, 2, Q, ROWS, BLOCK)
        o_copy(s).start()
        own4[:, pl.ds((core * CAP + s) * Q, Q)] = res[s, core]

    def handed(src, count, first, half):
        return [src, out.at[half, :, pl.ds(first, count)]]

    def f_here(b):
        src, dst = handed(arecv.at[:, pl.ds(b * B, B)], B, b * B, core)
        return pltpu.make_async_copy(src, dst, f_local.at[0])

    def f_mate(b):
        src, dst = handed(arecv.at[:, pl.ds(b * B, B)], B, b * B, core)
        return remote(src, dst, f_send.at[0], f_recv.at[0], peer)

    def spread(b):
        f_here(b).start()
        f_mate(b).start()

    for s in range(CAP):
        o_arrive(s).wait_recv()
    for way in range(2):
        for i in range(Z):
            shadow[way, i] = own4[way, ag_ref[i]]
    src, dst = handed(own4, 2 * CAP * Q, M, core)
    t_here = pltpu.make_async_copy(src, dst, t_local.at[0])
    t_mate = remote(src, dst, t_send.at[0], t_recv.at[0], peer)
    t_here.start()
    t_mate.start()

    stream(a_copy, arecv, lambda way, j: shadow[way, Z + j - lag_ref[2]], spread)

    for way in range(2):
        remote(ssend.at[way], arecv.at[way], a_send.at[way], a_recv.at[way, 0], z_to[way]).wait_send()
    src, dst = handed(arecv, M, 0, core)
    pltpu.make_async_copy(src, dst, f_local.at[0]).wait()
    remote(src, dst, f_send.at[0], f_recv.at[0], peer).wait_send()
    src, dst = handed(arecv, M, 0, mate)
    remote(src, dst, f_send.at[0], f_recv.at[0], peer).wait_recv()
    t_here.wait()
    t_mate.wait_send()
    src, dst = handed(own4, 2 * CAP * Q, M, mate)
    remote(src, dst, t_send.at[0], t_recv.at[0], peer).wait_recv()
    for buf, send, to in ((hb, x_send, x_to), (gb, y_send, y_to)):
        sent = buf.at[:, pl.ds(0, 3 * TOK)]
        remote(sent, sent, send.at[0], send.at[0], to[0]).wait_send()
    remote(pb.at[:, mate], eb, pe_send.at[0], pe_recv.at[0], peer).wait_send()
    for s in range(CAP):
        gx_copy(s).wait_send()
        o_copy(s).wait_send()


def run_main(owners, hidden, grad_out, left_stat, right_stat, left_root, right_root):
    dma = pltpu.SemaphoreType.DMA
    anywhere = pl.BlockSpec(memory_space=pl.ANY)
    scalars = pl.BlockSpec(memory_space=pltpu.SMEM)
    stream = pltpu.VMEM((2, M, ROWS, BLOCK), BF16)

    def table(size):
        return pltpu.SMEM((size,), jnp.int32)

    return pl.pallas_call(
        main_kernel,
        out_shape=(
            jax.ShapeDtypeStruct((2, 2, M + 2 * CAP * Q, ROWS, BLOCK), BF16),
            jax.ShapeDtypeStruct((2 * NB,), jnp.int32),
        ),
        in_specs=[scalars] + [anywhere] * 6,
        out_specs=(anywhere, scalars),
        scratch_shapes=[
            pltpu.VMEM((BR, 4 * TOK, BLOCK), BF16),
            pltpu.VMEM((BC, 4 * TOK, BLOCK), BF16),
            pltpu.VMEM((NB, 2, 2 * Q, ROWS, BLOCK), BF16),
            pltpu.VMEM((NB, 2 * Q, ROWS, BLOCK), BF16),
            pltpu.VMEM((2, NB * Q, ROWS, BLOCK), BF16),
            stream,
            stream,
            stream,
            pltpu.VMEM((2, Z + M, ROWS, BLOCK), BF16),
            pltpu.VMEM((CAP, 2, 2 * Q, ROWS, BLOCK), BF16),
            pltpu.VMEM((CAP, 2 * Q, ROWS, BLOCK), BF16),
            pltpu.VMEM((2, 2 * CAP * Q, ROWS, BLOCK), BF16),
            pltpu.VMEM((CAP, 2, 2, Q, ROWS, BLOCK), BF16),
            pltpu.VMEM((4, CAP, BLOCK, BLOCK), BF16),
            pltpu.VMEM((CAP, 4, BLOCK, BLOCK), BF16),
            pltpu.VMEM((CAP, BLOCK, BLOCK), F32),
            table(CHIPS), table(CHIPS), table(2 * M), table(4 * CAP), table(2 * CAP), table(Z), table(3),
            dma((11,)),
            dma((1,)), dma((BR, 4)), dma((1,)), dma((BC, 4)),
            dma((1,)), dma((NB,)),
            dma((2,)), dma((2, M)), dma((2,)), dma((2, M)),
            dma((CAP,)), dma((CAP,)), dma((CAP,)), dma((CAP,)),
            dma((1,)), dma((1,)), dma((1,)),
            dma((1,)), dma((1,)), dma((1,)),
        ],
        compiler_params=pltpu.CompilerParams(
            collective_id=0, has_side_effects=True, vmem_limit_bytes=62 * 1024 * 1024
        ),
        name="main",
    )(owners, hidden, grad_out, left_stat, right_stat, left_root, right_root)


def lay_out_kernel(pos, pieces, out, buf, in_sem, out_sem):
    def reads(k):
        return [
            pltpu.make_async_copy(
                pieces.at[half, way, pl.ds(pos[way * NB + k], Q)], buf.at[k, half, way], in_sem.at[k, half, way]
            )
            for half in range(2)
            for way in range(2)
        ]

    def write(k):
        r, c = k // BC, k % BC
        return pltpu.make_async_copy(
            buf.at[k].reshape(BLOCK, BLOCK),
            out.at[pl.ds(r * BLOCK, BLOCK), pl.ds(c * BLOCK, BLOCK)],
            out_sem.at[k],
        )

    for k in range(NB):
        for copy in reads(k):
            copy.start()
    for k in range(NB):
        for copy in reads(k):
            copy.wait()
        write(k).start()
    for k in range(NB):
        write(k).wait()


def run_lay_out(pos, pieces):
    dma = pltpu.SemaphoreType.DMA
    return pl.pallas_call(
        lay_out_kernel,
        out_shape=jax.ShapeDtypeStruct((BR * BLOCK, BC * BLOCK), BF16),
        in_specs=[pl.BlockSpec(memory_space=pltpu.SMEM), pl.BlockSpec(memory_space=pl.ANY)],
        out_specs=pl.BlockSpec(memory_space=pl.ANY),
        scratch_shapes=[
            pltpu.VMEM((NB, 2, 2, Q, ROWS, BLOCK), BF16),
            dma((NB, 2, 2)),
            dma((NB,)),
        ],
        compiler_params=pltpu.CompilerParams(vmem_limit_bytes=60 * 1024 * 1024),
        name="lay_out",
    )(pos, pieces)


def shards(hidden, grad_out, block_owner, left_stat, right_stat, left_root, right_root):
    pieces, pos = run_main(
        block_owner.reshape(NB), hidden, grad_out, left_stat, right_stat, left_root, right_root
    )
    return run_lay_out(pos, pieces)


def solution(mesh):
    in_specs = (
        P(("dp", "pre"), "mp"),
        P(("dp", "mp"), "pre"),
        P("mp", "pre", None, None),
        P("dp", "mp", "pre"),
        P("dp", "mp", "pre"),
        P("dp", "mp", "pre"),
        P("dp", "mp", "pre"),
    )
    return jax.shard_map(
        shards, mesh=mesh, in_specs=in_specs, out_specs=P("mp", "pre"), check_vma=False
    )
```

time: 214 us -> 177 us (0.83)
  Pallas kernels: 203 us -> 177 us
  local copies, waits for them, and re-layouts: 7.12 us -> 0 us
  other arithmetic: 3.51 us -> 0 us
    pallas_call x1, Pallas kernels: 198 us -> 170 us  [run_main(): pl.pallas_call(main_kernel, out_shape=(jax.ShapeDtypeStruct((2, 2, M + 2...]
    unnamed x2 -> x0, local copies, waits for them, and re-layouts: 3.97 us -> none
    concatenate x1 -> x0, local copies, waits for them, and re-layouts: 2.56 us -> none  [tables(): table = jnp.concatenate(rs + rslag + fin + [kslot, ag, own_places[None]])]
    reduce_sum x8 -> x0, other arithmetic: 2.35 us -> none  [the longest x1 0.91 us: tables(): slot = jnp.sum(same_owner.astype(jnp.int32), axis=1)]
where the time goes in v2:
time: 177 us
  Pallas kernels  177 us (100%)
    pallas_call x1, Pallas kernels, run_main(): pl.pallas_call(main_kernel, out_shape=(jax.ShapeDtypeStruct((2, 2, M + 2...  170 us
    pallas_call x1, Pallas kernels, run_lay_out(): pl.pallas_call(lay_out_kernel, out_shape=jax.ShapeDtypeStruct((BR * BLOCK...  6.53 us

profile of v2, /device:TPU:1, one launch (start us, length us, event | category | flops | bytes accessed | tf_op | source)
XLA Modules:
  0.0 177.1 jit_solution(1574579181739053914)
XLA Ops:
  0.0 170.4 %main.1 = (bf16[2,2,44,64,512]{4,3,2,1,0:T(8,128)(2,1)}, s32[24]{0:T(128)}) custom-call(s32[12]{0:T(128)} %bitcast.1, bf16[256,1536]{1,0:T(8,128)(2,1)} %hid.1, bf16[256,2048]{1,0:T(8,128)(2,1)} %gro.1, bf16[2,512,512]{2,1,0:T(8,128)(2,1)} %ls.1, bf16[2,512,512]{2,1,0:T(8,128)(2,1)} %rs.1, bf16[2,512,512]{2,1,0:T(8,128)(2,1)} %lr.1, bf16[2,512,512]{2,1,0:T(8,128)(2,1)} %rr.1), custom_call_target="tpu_custom_call" | custom-call | tf_op jit(solution)/shard_map/main/pallas_call | solution.py:420
  170.4 6.5 %lay_out.1 = bf16[1536,2048]{1,0:T(8,128)(2,1)} custom-call(s32[24]{0:T(128)} %get-tuple-element.7.pos, bf16[2,2,44,64,512]{4,3,2,1,0:T(8,128)(2,1)} %get-tuple-element.8.pieces), custom_call_target="tpu_custom_call" | custom-call | tf_op jit(solution)/shard_map/lay_out/pallas_call | solution.py:492

commit v3 on v2

--- a/solution.py
+++ b/solution.py
@@ -17,8 +17,8 @@
 CHIPS = 8
 TOK = 256
 
-Q = 2
-U = 3
+Q = 4
+U = 5
 ROWS = BLOCK // 4 // Q
 Z = max(2 * CAP * Q, U)
 M = NB * Q + 4 * U
@@ -112,7 +112,7 @@
 
 def main_kernel(
     owner_ref, hid, gro, ls, rs, lr, rr, out, pos_ref,
-    hb, gb, pb, eb, sb, ssend, srecv, arecv, shadow, gfull, gx, own4, res, stats, ops, cf,
+    hb, gb, pb, eb, sb, ssend, srecv, arecv, shadow, gfull, gx, own4, res, stats, ops, cf, acc,
     places_ref, before_ref, rs_ref, fin_ref, kslot_ref, ag_ref, lag_ref,
     local_sem, x_send, x_recv, y_send, y_recv, pe_send, pe_recv,
     s_send, s_recv, a_send, a_recv, gx_send, gx_recv, o_send, o_recv,
@@ -204,11 +204,11 @@
                     arrived(i, way).wait_recv()
                     forward(i, way).start()
 
-    def finish(i):
-        for count, (_, _, _, far) in rings:
-            if i < count:
-                for way in range(2):
-                    far(i, way).wait_recv()
+    def finish(i, which):
+        count, (_, _, _, far) = rings[which]
+        if i < count:
+            for way in range(2):
+                far(i, way).wait_recv()
 
     def operators(side, s):
         a, b = fifth(stats[2 + side, s], stats[side, s])
@@ -222,11 +222,22 @@
     def to_mate(k):
         return remote(pb.at[k, mate], eb.at[k], pe_send.at[0], pe_recv.at[k], peer)
 
+    def store(k, value):
+        pb[k] = value.astype(BF16).reshape(2, 2 * Q, ROWS, BLOCK)
+        to_mate(k).start()
+
     def partial(r, c):
-        k = r * BC + c
-        value = mm_t(hb[r], gb[c]).astype(BF16)
-        pb[k] = value.reshape(2, 2 * Q, ROWS, BLOCK)
-        to_mate(k).start()
+        store(r * BC + c, mm_t(hb[r], gb[c]))
+
+    def part(r, c, step):
+        rows = pl.ds(lax.rem(mp + step, 4) * TOK, TOK)
+        return mm_t(hb[r, rows], gb[c, rows])
+
+    def early(r, c):
+        acc[r] = part(r, c, 0) + part(r, c, 1) + part(r, c, 3)
+
+    def late(r, c):
+        store(r * BC + c, acc[r] + part(r, c, 2))
 
     def add_halves(r, c):
         k = r * BC + c
@@ -235,47 +246,47 @@
             both = pb[k, core, pl.ds(way * Q, Q)].astype(F32) + eb[k, pl.ds(way * Q, Q)].astype(F32)
             sb[way, pl.ds(k * Q, Q)] = both.astype(BF16)
 
-    def for_chunk(i, what):
-        if i < BR:
-            lax.fori_loop(0, i + 1, lambda c, _: (what(i, c), 0)[1], 0)
-        if i > 0:
-            lax.fori_loop(0, min(i, BR), lambda r, _: (what(r, i), 0)[1], 0)
-
-    def between(i):
-        if i == 0:
-            for copy in stat_copies:
-                copy.wait()
-            operators(0, 0)
-        elif i == 1:
-            operators(1, 0)
-            for way in range(2):
-                shadow[way, pl.ds(0, Z)] = jnp.zeros((Z, ROWS, BLOCK), BF16)
-        elif i == 2:
-            make_tables(
-                owner_ref, chip, places_ref, before_ref, rs_ref, fin_ref, kslot_ref, ag_ref, lag_ref, pos_ref
-            )
-            operators(0, 1)
-        elif i == 3:
-            operators(1, 1)
+    def rows_of(c, what, count=BR):
+        lax.fori_loop(0, count, lambda r, _: (what(r, c), 0)[1], 0)
 
     start_direct(0)
     start_direct(1)
-    for copy in token_copies:
+    for copy in token_copies + stat_copies:
         copy.wait()
-    between(0)
-    for i in range(BC + 1):
-        if i < BC:
-            pass_on(i)
-            if i + 2 < BC:
-                start_direct(i + 2)
-            if i + 1 < BC:
-                between(i + 1)
-        if i > 0:
-            finish(i - 1)
-            for_chunk(i - 1, partial)
-        if i > 1:
-            for_chunk(i - 2, add_halves)
-    for_chunk(BC - 1, add_halves)
+    operators(0, 0)
+    operators(1, 0)
+    pass_on(0)
+    start_direct(2)
+    operators(0, 1)
+    for way in range(2):
+        shadow[way, pl.ds(0, Z)] = jnp.zeros((Z, ROWS, BLOCK), BF16)
+    pass_on(1)
+    start_direct(3)
+    operators(1, 1)
+    finish(0, 0)
+    finish(0, 1)
+    partial(0, 0)
+    make_tables(
+        owner_ref, chip, places_ref, before_ref, rs_ref, fin_ref, kslot_ref, ag_ref, lag_ref, pos_ref
+    )
+    pass_on(2)
+    finish(1, 0)
+    finish(1, 1)
+    rows_of(1, partial, 2)
+    partial(1, 0)
+    finish(2, 0)
+    lax.fori_loop(0, 2, lambda c, _: (partial(2, c), 0)[1], 0)
+    pass_on(3)
+    rows_of(2, early)
+    finish(2, 1)
+    rows_of(2, late)
+    rows_of(3, early)
+    for c in range(2):
+        rows_of(c, add_halves)
+    finish(3, 1)
+    rows_of(3, late)
+    for c in range(2, BC):
+        rows_of(c, add_halves)
 
     def s_copy(way, j):
         return remote(ssend.at[way, j], srecv.at[way, j], s_send.at[way], s_recv.at[way, j], z_to[way])
@@ -347,14 +358,16 @@
         place = mate * CAP + s
         return remote(res.at[s, mate], own4.at[:, pl.ds(place * Q, Q)], o_send.at[s], o_recv.at[s], peer)
 
-    for s in range(CAP):
+    both = range(CAP)
+    for s in both:
         gx_arrive(s).wait_recv()
-        g = gfull[s].reshape(BLOCK, BLOCK)
-        gram = mm_t(g, g).astype(BF16)
-        cube = mm(g, gram).astype(BF16)
-        m = mm(ops[s, 0], g) + mm(ops[s, 1], g) - mm(ops[s, 2], cube)
-        n = cf[s] - mm(ops[s, 3], gram)
-        p = mm(m.astype(BF16), n.astype(BF16))
+    g = [gfull[s].reshape(BLOCK, BLOCK) for s in both]
+    gram = [mm_t(g[s], g[s]).astype(BF16) for s in both]
+    cube = [mm(g[s], gram[s]).astype(BF16) for s in both]
+    m = [(mm(ops[s, 0], g[s]) + mm(ops[s, 1], g[s]) - mm(ops[s, 2], cube[s])).astype(BF16) for s in both]
+    n = [(cf[s] - mm(ops[s, 3], gram[s])).astype(BF16) for s in both]
+    for s in both:
+        p = mm(m[s], n[s])
         inv = lax.rsqrt(jnp.sum(p * p, keepdims=True) * (1.0 / (BLOCK * BLOCK)) + 1e-06)
         res[s] = (p * inv).astype(BF16).reshape(2, 2, Q, ROWS, BLOCK)
         o_copy(s).start()
@@ -442,6 +455,7 @@
             pltpu.VMEM((4, CAP, BLOCK, BLOCK), BF16),
             pltpu.VMEM((CAP, 4, BLOCK, BLOCK), BF16),
             pltpu.VMEM((CAP, BLOCK, BLOCK), F32),
+            pltpu.VMEM((BR, BLOCK, BLOCK), F32),
             table(CHIPS), table(CHIPS), table(2 * M), table(4 * CAP), table(2 * CAP), table(Z), table(3),
             dma((11,)),
             dma((1,)), dma((BR, 4)), dma((1,)), dma((BC, 4)),

time: 177 us -> 170 us (0.960)
  Pallas kernels: 177 us -> 169 us
    pallas_call x1, Pallas kernels: 170 us -> 163 us  [run_main(): pl.pallas_call(main_kernel, out_shape=(jax.ShapeDtypeStruct((2, 2, M + 2...]
where the time goes in v3:
time: 170 us
  Pallas kernels  169 us (99%)
    pallas_call x1, Pallas kernels, run_main(): pl.pallas_call(main_kernel, out_shape=(jax.ShapeDtypeStruct((2, 2, M + 2...  163 us
    pallas_call x1, Pallas kernels, run_lay_out(): pl.pallas_call(lay_out_kernel, out_shape=jax.ShapeDtypeStruct((BR * BLOCK...  6.53 us

profile of v3, /device:TPU:1, one launch (start us, length us, event | category | flops | bytes accessed | tf_op | source)
XLA Modules:
  0.0 169.6 jit_solution(552672912752782650)
XLA Ops:
  0.0 162.9 %main.1 = (bf16[2,2,84,32,512]{4,3,2,1,0:T(8,128)(2,1)}, s32[24]{0:T(128)}) custom-call(s32[12]{0:T(128)} %bitcast.1, bf16[256,1536]{1,0:T(8,128)(2,1)} %hid.1, bf16[256,2048]{1,0:T(8,128)(2,1)} %gro.1, bf16[2,512,512]{2,1,0:T(8,128)(2,1)} %ls.1, bf16[2,512,512]{2,1,0:T(8,128)(2,1)} %rs.1, bf16[2,512,512]{2,1,0:T(8,128)(2,1)} %lr.1, bf16[2,512,512]{2,1,0:T(8,128)(2,1)} %rr.1), custom_call_target="tpu_custom_call" | custom-call | tf_op jit(solution)/shard_map/main/pallas_call | solution.py:433
  162.9 6.5 %lay_out.1 = bf16[1536,2048]{1,0:T(8,128)(2,1)} custom-call(s32[24]{0:T(128)} %get-tuple-element.7.pos, bf16[2,2,84,32,512]{4,3,2,1,0:T(8,128)(2,1)} %get-tuple-element.8.pieces), custom_call_target="tpu_custom_call" | custom-call | tf_op jit(solution)/shard_map/lay_out/pallas_call | solution.py:506

commit v4 on v3

--- a/solution.py
+++ b/solution.py
@@ -22,6 +22,7 @@
 ROWS = BLOCK // 4 // Q
 Z = max(2 * CAP * Q, U)
 M = NB * Q + 4 * U
+R = min(M, CHIPS * U)
 B = 4
 assert M % B == 0 and Q * 2 >= U
 
@@ -289,10 +290,10 @@
         rows_of(c, add_halves)
 
     def s_copy(way, j):
-        return remote(ssend.at[way, j], srecv.at[way, j], s_send.at[way], s_recv.at[way, j], z_to[way])
+        return remote(ssend.at[way, j], srecv.at[way, j], s_send.at[way], s_recv.at[way, lax.rem(j, R)], z_to[way])
 
     def a_copy(way, j):
-        return remote(ssend.at[way, j], arecv.at[way, j], a_send.at[way], a_recv.at[way, j], z_to[way])
+        return remote(ssend.at[way, j], arecv.at[way, j], a_send.at[way], a_recv.at[way, lax.rem(j, R)], z_to[way])
 
     def stream(copy, landed, message, after):
         def step(j, send):
@@ -460,7 +461,7 @@
             dma((11,)),
             dma((1,)), dma((BR, 4)), dma((1,)), dma((BC, 4)),
             dma((1,)), dma((NB,)),
-            dma((2,)), dma((2, M)), dma((2,)), dma((2, M)),
+            dma((2,)), dma((2, R)), dma((2,)), dma((2, R)),
             dma((CAP,)), dma((CAP,)), dma((CAP,)), dma((CAP,)),
             dma((1,)), dma((1,)), dma((1,)),
             dma((1,)), dma((1,)), dma((1,)),

time: 170 us -> 169 us (level)
  no operation moved by 1% of the time
where the time goes in v4:
time: 169 us
  Pallas kernels  168 us (99%)
    pallas_call x1, Pallas kernels, run_main(): pl.pallas_call(main_kernel, out_shape=(jax.ShapeDtypeStruct((2, 2, M + 2...  162 us
    pallas_call x1, Pallas kernels, run_lay_out(): pl.pallas_call(lay_out_kernel, out_shape=jax.ShapeDtypeStruct((BR * BLOCK...  6.53 us

profile of v4, /device:TPU:1, one launch (start us, length us, event | category | flops | bytes accessed | tf_op | source)
XLA Modules:
  0.0 168.6 jit_solution(17230220509806123005)
XLA Ops:
  0.0 161.9 %main.1 = (bf16[2,2,84,32,512]{4,3,2,1,0:T(8,128)(2,1)}, s32[24]{0:T(128)}) custom-call(s32[12]{0:T(128)} %bitcast.1, bf16[256,1536]{1,0:T(8,128)(2,1)} %hid.1, bf16[256,2048]{1,0:T(8,128)(2,1)} %gro.1, bf16[2,512,512]{2,1,0:T(8,128)(2,1)} %ls.1, bf16[2,512,512]{2,1,0:T(8,128)(2,1)} %rs.1, bf16[2,512,512]{2,1,0:T(8,128)(2,1)} %lr.1, bf16[2,512,512]{2,1,0:T(8,128)(2,1)} %rr.1), custom_call_target="tpu_custom_call" | custom-call | tf_op jit(solution)/shard_map/main/pallas_call | solution.py:434
  161.9 6.5 %lay_out.1 = bf16[1536,2048]{1,0:T(8,128)(2,1)} custom-call(s32[24]{0:T(128)} %get-tuple-element.7.pos, bf16[2,2,84,32,512]{4,3,2,1,0:T(8,128)(2,1)} %get-tuple-element.8.pieces), custom_call_target="tpu_custom_call" | custom-call | tf_op jit(solution)/shard_map/lay_out/pallas_call | solution.py:507
